TPU v7x, 256 devices: a whole 4x4x8 slice. The times are simulated.
256 devices in a mesh: ctx: 64 (over y, z, core), tp: 4 (over x).
Axes of the slice: x: 4, y: 4, z: 8, core: 2. Of those that a mesh axis runs over, the one named last changes fastest.
Arguments:
- gate_branch: bfloat16 [8192, 4096], P('ctx', 'tp'), may hold values from -520 to 520
- key_branch: bfloat16 [8192, 4096], P('ctx', 'tp'), may hold values from -6 to 6
- value_branch: bfloat16 [8192, 4096], P('ctx', 'tp'), may hold values from -6 to 6
- spectrum_real: float32 [128, 128, 4096], P(None, 'ctx', 'tp'), may hold values from -6 to 6
- spectrum_imag: float32 [128, 128, 4096], P(None, 'ctx', 'tp'), may hold values from -6 to 6
- norm_gain: float32 [4096], P('tp'), may hold values from 0.1 to 1.9
Outputs:
- mixed: bfloat16 [8192, 4096], P('ctx', 'tp')
All inputs are finite; a program needn't handle non-finite values.
Results may differ from a plain program's by a relative error of at most 0.001.
Values sent between devices are 32-bit elements; how exact they have to be, the bound alone decides.
A program may use at most 64 MiB of HBM per device.

v0:
```python
import math

import jax
import jax.numpy as jnp
from jax import lax
from jax.sharding import PartitionSpec as P

epsilon = 1e-05
highest = lax.Precision.HIGHEST


def swapped(array, axis, distance):
    return lax.ppermute(array, axis, [(i, i ^ 1 << distance) for i in range(lax.axis_size(axis))])


def reversed_bits(values, count_bits):
    result = values * 0
    for bit_level in range(count_bits):
        result = result | (values >> bit_level & 1) << count_bits - 1 - bit_level
    return result


def rotate(real_part, imag_part, angles):
    cosines = jnp.cos(angles)
    sines = jnp.sin(angles)
    return (real_part * cosines - imag_part * sines, real_part * sines + imag_part * cosines)


def local(gate_branch, key_branch, value_branch, spectrum_real, spectrum_imag, norm_gain):
    devices = lax.axis_size("ctx")
    my_index = lax.axis_index("ctx")
    count_bits = devices.bit_length() - 1
    tok_count = key_branch.shape[0]
    chan_count = key_branch.shape[1]
    fft_length = 2 * tok_count * devices
    two_pi = 2.0 * math.pi
    signal = key_branch.astype(jnp.float32) * value_branch.astype(jnp.float32)
    own_angle = -(two_pi / (2 * devices)) * my_index.astype(jnp.float32)
    odd_real = signal * jnp.cos(own_angle)
    odd_imag = signal * jnp.sin(own_angle)
    carried = jnp.stack(
        [jnp.stack([signal, odd_real]), jnp.stack([jnp.zeros_like(signal), odd_imag])]
    )
    for bit_level in range(count_bits - 1, -1, -1):
        half_span = 1 << bit_level
        partner = swapped(carried, "ctx", bit_level)
        is_upper = my_index >> bit_level & 1
        flip_sign = (1 - 2 * is_upper).astype(jnp.float32)
        angles = -(two_pi / (2 * half_span)) * ((my_index & half_span - 1) * is_upper).astype(
            jnp.float32
        )
        combined = partner + flip_sign * carried
        new_real, new_imag = rotate(combined[0], combined[1], angles)
        carried = jnp.stack([new_real, new_imag])
    part_real = carried[0]
    part_imag = carried[1]
    freq_local = 2 * reversed_bits(my_index, count_bits) + jnp.arange(2, dtype=jnp.int32)
    positions = jnp.arange(tok_count, dtype=jnp.int32)
    twist_ids = freq_local[:, None] * positions[None, :] % fft_length
    twist = two_pi / fft_length * twist_ids.astype(jnp.float32)
    rotated_real, rotated_imag = rotate(part_real, part_imag, -twist[:, :, None])
    table_ids = positions[:, None] * positions[None, :] % tok_count
    table_angle = two_pi / tok_count * table_ids.astype(jnp.float32)
    dft_cos = jnp.cos(table_angle)
    dft_sin = jnp.sin(table_angle)
    freq_real = jnp.einsum("kb,ebc->kec", dft_cos, rotated_real, precision=highest) + jnp.einsum(
        "kb,ebc->kec", dft_sin, rotated_imag, precision=highest
    )
    freq_imag = jnp.einsum("kb,ebc->kec", dft_cos, rotated_imag, precision=highest) - jnp.einsum(
        "kb,ebc->kec", dft_sin, rotated_real, precision=highest
    )
    prod_real = freq_real * spectrum_real - freq_imag * spectrum_imag
    prod_imag = freq_real * spectrum_imag + freq_imag * spectrum_real
    back_real = jnp.einsum("bk,kec->ebc", dft_cos, prod_real, precision=highest) - jnp.einsum(
        "bk,kec->ebc", dft_sin, prod_imag, precision=highest
    )
    back_imag = jnp.einsum("bk,kec->ebc", dft_cos, prod_imag, precision=highest) + jnp.einsum(
        "bk,kec->ebc", dft_sin, prod_real, precision=highest
    )
    back_real, back_imag = rotate(back_real, back_imag, twist[:, :, None])
    carried = jnp.stack([back_real, back_imag])
    for bit_level in range(count_bits):
        half_span = 1 << bit_level
        is_upper = my_index >> bit_level & 1
        flip_sign = (1 - 2 * is_upper).astype(jnp.float32)
        angles = (
            two_pi / (2 * half_span) * ((my_index & half_span - 1) * is_upper).astype(jnp.float32)
        )
        prep_real, prep_imag = rotate(carried[0], carried[1], angles)
        prepared = jnp.stack([prep_real, prep_imag])
        partner = swapped(prepared, "ctx", bit_level)
        carried = partner + flip_sign * prepared
    final_angle = two_pi / (2 * devices) * my_index.astype(jnp.float32)
    convolved = (
        carried[0, 0] + jnp.cos(final_angle) * carried[0, 1] - jnp.sin(final_angle) * carried[1, 1]
    ) / fft_length
    gated = gate_branch.astype(jnp.float32) * convolved
    local_sum = jnp.sum(gated * gated, axis=1)
    channel_total = lax.psum(local_sum, "tp")
    mean_square = channel_total / (chan_count * lax.axis_size("tp"))
    return (gated * lax.rsqrt(mean_square + epsilon)[:, None] * norm_gain[None, :]).astype(
        jnp.bfloat16
    )


def solution(mesh):
    in_specs = (
        P("ctx", "tp"),
        P("ctx", "tp"),
        P("ctx", "tp"),
        P(None, "ctx", "tp"),
        P(None, "ctx", "tp"),
        P("tp"),
    )
    out_specs = P("ctx", "tp")
    return jax.shard_map(local, mesh=mesh, in_specs=in_specs, out_specs=out_specs, check_vma=False)
```

profile of v0, /device:TPU:1, one launch (start us, length us, event | category | flops | bytes accessed | tf_op | source)
XLA Modules:
  0.0 741.9 jit_solution(10255638031382982681)
XLA Ops:
  4.1 3.7 collective-permute-start
  8.0 44.5 %collective-permute-done = f32[2,2,128,1024]{2,3,1,0:T(8,128)} collective-permute-done((f32[2,2,128,1024]{2,3,1,0:T(8,128)}, f32[2,2,128,1024]{2,3,1,0:T(8,128)}, u32[]{:S(2)}, u32[]{:S(2)}) %collective-permute-start) | collective-permute-done | bytes 2097184 | tf_op jit(solution)/shard_map/ppermute | solution.py:13
  56.0 2.1 collective-permute-start.1
  58.2 44.2 %collective-permute-done.1 = f32[2,2,128,1024]{2,3,1,0:T(8,128)} collective-permute-done((f32[2,2,128,1024]{2,3,1,0:T(8,128)}, f32[2,2,128,1024]{2,3,1,0:T(8,128)}, u32[]{:S(2)}, u32[]{:S(2)}) %collective-permute-start.1) | collective-permute-done | bytes 2097184 | tf_op jit(solution)/shard_map/ppermute | solution.py:13
  105.9 7.2 collective-permute-start.2
  113.2 57.9 %collective-permute-done.2 = f32[2,2,128,1024]{2,3,1,0:T(8,128)} collective-permute-done((f32[2,2,128,1024]{2,3,1,0:T(8,128)}, f32[2,2,128,1024]{2,3,1,0:T(8,128)}, u32[]{:S(2)}, u32[]{:S(2)}) %collective-permute-start.2) | collective-permute-done | bytes 2097184 | tf_op jit(solution)/shard_map/ppermute | solution.py:13
  174.6 34.1 %collective-permute-start.3 = (f32[2,2,128,1024]{2,3,1,0:T(8,128)}, f32[2,2,128,1024]{2,3,1,0:T(8,128)}, u32[]{:S(2)}, u32[]{:S(2)}) collective-permute-start(f32[2,2,128,1024]{2,3,1,0:T(8,128)} %pad_maximum_fusion.3), channel_id=1, source_target_pairs={{0,16},{4,20},{8,24},{12,28},{16,0},{20,4},{24,8},{28,12},{32,48},... | collective-permute-start | bytes 6291464 | tf_op jit(solution)/shard_map/ppermute | solution.py:13
  208.8 90.8 %collective-permute-done.3 = f32[2,2,128,1024]{2,3,1,0:T(8,128)} collective-permute-done((f32[2,2,128,1024]{2,3,1,0:T(8,128)}, f32[2,2,128,1024]{2,3,1,0:T(8,128)}, u32[]{:S(2)}, u32[]{:S(2)}) %collective-permute-start.3) | collective-permute-done | bytes 2097184 | tf_op jit(solution)/shard_map/ppermute | solution.py:13
  303.3 46.4 %collective-permute-done.4 = f32[2,2,128,1024]{2,3,1,0:T(8,128)} collective-permute-done((f32[2,2,128,1024]{2,3,1,0:T(8,128)}, f32[2,2,128,1024]{2,3,1,0:T(8,128)}, u32[]{:S(2)}, u32[]{:S(2)}) %collective-permute-start.4) | collective-permute-done | bytes 2097184 | tf_op jit(solution)/shard_map/ppermute | solution.py:13
  355.2 4.0 collective-permute-done.5
  365.3 2.0 multiply_subtract_fusion.6
  367.2 1.9 fusion.18
  369.2 1.9 fusion.20
  371.1 2.2 convolution_add_fusion
  373.3 2.1 fusion.1
  377.4 4.0 collective-permute-done.6
  385.0 47.0 %collective-permute-done.7 = f32[2,2,128,1024]{2,3,1,0:T(8,128)} collective-permute-done((f32[2,2,128,1024]{2,3,1,0:T(8,128)}, f32[2,2,128,1024]{2,3,1,0:T(8,128)}, u32[]{:S(2)}, u32[]{:S(2)}) %collective-permute-start.7) | collective-permute-done | bytes 2097184 | tf_op jit(solution)/shard_map/ppermute | solution.py:13
  435.7 93.3 %collective-permute-done.8 = f32[2,2,128,1024]{2,3,1,0:T(8,128)} collective-permute-done((f32[2,2,128,1024]{2,3,1,0:T(8,128)}, f32[2,2,128,1024]{2,3,1,0:T(8,128)}, u32[]{:S(2)}, u32[]{:S(2)}) %collective-permute-start.8) | collective-permute-done | bytes 2097184 | tf_op jit(solution)/shard_map/ppermute | solution.py:13
  532.5 3.2 collective-permute-start.9
  535.9 93.2 %collective-permute-done.9 = f32[2,2,128,1024]{2,3,1,0:T(8,128)} collective-permute-done((f32[2,2,128,1024]{2,3,1,0:T(8,128)}, f32[2,2,128,1024]{2,3,1,0:T(8,128)}, u32[]{:S(2)}, u32[]{:S(2)}) %collective-permute-start.9) | collective-permute-done | bytes 2097184 | tf_op jit(solution)/shard_map/ppermute | solution.py:13
  634.0 45.4 %collective-permute-done.10 = f32[2,2,128,1024]{2,3,1,0:T(8,128)} collective-permute-done((f32[2,2,128,1024]{2,3,1,0:T(8,128)}, f32[2,2,128,1024]{2,3,1,0:T(8,128)}, u32[]{:S(2)}, u32[]{:S(2)}) %collective-permute-start.10) | collective-permute-done | bytes 2097184 | tf_op jit(solution)/shard_map/ppermute | solution.py:13
  682.9 2.9 collective-permute-start.11
  686.1 44.2 %collective-permute-done.11 = f32[2,2,128,1024]{2,3,1,0:T(8,128)} collective-permute-done((f32[2,2,128,1024]{2,3,1,0:T(8,128)}, f32[2,2,128,1024]{2,3,1,0:T(8,128)}, u32[]{:S(2)}, u32[]{:S(2)}) %collective-permute-start.11) | collective-permute-done | bytes 2097184 | tf_op jit(solution)/shard_map/ppermute | solution.py:13
  732.3 8.5 %psum.7 = f32[128]{0:T(128)S(1)} all-reduce(f32[128]{0:T(128)S(1)} %get-tuple-element.5), channel_id=1, replica_groups=mesh['ctx'=64,'tp'=4] {'tp'}, use_global_device_ids=true, to_apply=%region_1.2 | all-reduce | flops 128 | bytes 1024 | tf_op jit(solution)/shard_map/psum | solution.py:99
  (63 shorter events, 53.1 us)
Async XLA Ops:
  4.1 48.4 %collective-permute-start = (f32[2,2,128,1024]{2,3,1,0:T(8,128)}, f32[2,2,128,1024]{2,3,1,0:T(8,128)}, u32[]{:S(2)}, u32[]{:S(2)}) collective-permute-start(f32[2,2,128,1024]{2,3,1,0:T(8,128)} %pad_maximum_fusion), channel_id=1, source_target_pairs={{0,128},{4,132},{8,136},{12,140},{16,144},{20,148},{24,152},{28,15... | collective-permute-start | bytes 6291464 | tf_op jit(solution)/shard_map/ppermute | solution.py:13
  56.0 46.4 %collective-permute-start.1 = (f32[2,2,128,1024]{2,3,1,0:T(8,128)}, f32[2,2,128,1024]{2,3,1,0:T(8,128)}, u32[]{:S(2)}, u32[]{:S(2)}) collective-permute-start(f32[2,2,128,1024]{2,3,1,0:T(8,128)} %pad_maximum_fusion.1), channel_id=1, source_target_pairs={{0,64},{4,68},{8,72},{12,76},{16,80},{20,84},{24,88},{28,92},{32,9... | collective-permute-start | bytes 6291464 | tf_op jit(solution)/shard_map/ppermute | solution.py:13
  105.9 65.2 %collective-permute-start.2 = (f32[2,2,128,1024]{2,3,1,0:T(8,128)}, f32[2,2,128,1024]{2,3,1,0:T(8,128)}, u32[]{:S(2)}, u32[]{:S(2)}) collective-permute-start(f32[2,2,128,1024]{2,3,1,0:T(8,128)} %pad_maximum_fusion.2), channel_id=1, source_target_pairs={{0,32},{4,36},{8,40},{12,44},{16,48},{20,52},{24,56},{28,60},{32,0... | collective-permute-start | bytes 6291464 | tf_op jit(solution)/shard_map/ppermute | solution.py:13
  174.6 125.0 %collective-permute-start.3 = (f32[2,2,128,1024]{2,3,1,0:T(8,128)}, f32[2,2,128,1024]{2,3,1,0:T(8,128)}, u32[]{:S(2)}, u32[]{:S(2)}) collective-permute-start(f32[2,2,128,1024]{2,3,1,0:T(8,128)} %pad_maximum_fusion.3), channel_id=1, source_target_pairs={{0,16},{4,20},{8,24},{12,28},{16,0},{20,4},{24,8},{28,12},{32,48},... | collective-permute-start | bytes 6291464 | tf_op jit(solution)/shard_map/ppermute | solution.py:13
  303.2 46.6 %collective-permute-start.4 = (f32[2,2,128,1024]{2,3,1,0:T(8,128)}, f32[2,2,128,1024]{2,3,1,0:T(8,128)}, u32[]{:S(2)}, u32[]{:S(2)}) collective-permute-start(f32[2,2,128,1024]{2,3,1,0:T(8,128)} %pad_maximum_fusion.4), channel_id=1, source_target_pairs={{0,8},{4,12},{8,0},{12,4},{16,24},{20,28},{24,16},{28,20},{32,40},... | collective-permute-start | bytes 6291464 | tf_op jit(solution)/shard_map/ppermute | solution.py:13
  353.3 5.9 collective-permute-start.5
  363.7 1.3 copy-start
  363.7 1.5 copy-start.1
  376.9 4.5 collective-permute-start.6
  384.9 47.2 %collective-permute-start.7 = (f32[2,2,128,1024]{2,3,1,0:T(8,128)}, f32[2,2,128,1024]{2,3,1,0:T(8,128)}, u32[]{:S(2)}, u32[]{:S(2)}) collective-permute-start(f32[2,2,128,1024]{2,3,1,0:T(8,128)} %pad_maximum_fusion.7), channel_id=1, source_target_pairs={{0,8},{4,12},{8,0},{12,4},{16,24},{20,28},{24,16},{28,20},{32,40},... | collective-permute-start | bytes 6291464 | tf_op jit(solution)/shard_map/ppermute | solution.py:13
  435.5 93.4 %collective-permute-start.8 = (f32[2,2,128,1024]{2,3,1,0:T(8,128)}, f32[2,2,128,1024]{2,3,1,0:T(8,128)}, u32[]{:S(2)}, u32[]{:S(2)}) collective-permute-start(f32[2,2,128,1024]{2,3,1,0:T(8,128)} %pad_maximum_fusion.8), channel_id=1, source_target_pairs={{0,16},{4,20},{8,24},{12,28},{16,0},{20,4},{24,8},{28,12},{32,48},... | collective-permute-start | bytes 6291464 | tf_op jit(solution)/shard_map/ppermute | solution.py:13
  532.5 96.6 %collective-permute-start.9 = (f32[2,2,128,1024]{2,3,1,0:T(8,128)}, f32[2,2,128,1024]{2,3,1,0:T(8,128)}, u32[]{:S(2)}, u32[]{:S(2)}) collective-permute-start(f32[2,2,128,1024]{2,3,1,0:T(8,128)} %pad_maximum_fusion.9), channel_id=1, source_target_pairs={{0,32},{4,36},{8,40},{12,44},{16,48},{20,52},{24,56},{28,60},{32,0... | collective-permute-start | bytes 6291464 | tf_op jit(solution)/shard_map/ppermute | solution.py:13
  632.5 46.9 %collective-permute-start.10 = (f32[2,2,128,1024]{2,3,1,0:T(8,128)}, f32[2,2,128,1024]{2,3,1,0:T(8,128)}, u32[]{:S(2)}, u32[]{:S(2)}) collective-permute-start(f32[2,2,128,1024]{2,3,1,0:T(8,128)} %pad_maximum_fusion.10), channel_id=1, source_target_pairs={{0,64},{4,68},{8,72},{12,76},{16,80},{20,84},{24,88},{28,92},{32,9... | collective-permute-start | bytes 6291464 | tf_op jit(solution)/shard_map/ppermute | solution.py:13
  681.4 4.6 copy-start.2
  682.9 47.4 %collective-permute-start.11 = (f32[2,2,128,1024]{2,3,1,0:T(8,128)}, f32[2,2,128,1024]{2,3,1,0:T(8,128)}, u32[]{:S(2)}, u32[]{:S(2)}) collective-permute-start(f32[2,2,128,1024]{2,3,1,0:T(8,128)} %pad_maximum_fusion.11), channel_id=1, source_target_pairs={{0,128},{4,132},{8,136},{12,140},{16,144},{20,148},{24,152},{28,15... | collective-permute-start | bytes 6291464 | tf_op jit(solution)/shard_map/ppermute | solution.py:13
  732.1 8.7 %copy-start.3 = (f32[1024]{0:T(1024)S(1)}, f32[1024]{0:T(1024)}, u32[]{:S(2)}) copy-start(f32[1024]{0:T(1024)} %param.11) | copy-start | bytes 12292
where the time goes:
time: 745 us; the launch traced here: 742 us
  waiting for transfers between devices  615 us (83%)
  starting transfers between devices  56.7 us (8%)
  other arithmetic  42.3 us (6%)
  matrix products  14 us (2%)
  blocking collectives  8.53 us (1%)
    ppermute x12, waiting for transfers between devices, swapped(): lax.ppermute(array, axis, [(i, i ^ 1 << distance) for i in range(lax.axis...  615 us
    ppermute x12, starting transfers between devices, swapped(): lax.ppermute(array, axis, [(i, i ^ 1 << distance) for i in range(lax.axis...  56.7 us
  transfers between devices with their start and end apart: 12, of which 12 were waited for; matrix products, arithmetic and copies ran while one was open for 0% of the time, Pallas kernels for 0%

commit v1 on v0

v1 whole, which is shorter than its diff:
```python
import functools

import jax
import jax.numpy as jnp
import ml_dtypes
import numpy as np
from jax import lax
from jax.experimental import pallas as pl
from jax.experimental.pallas import tpu as pltpu
from jax.sharding import PartitionSpec as P

MESH = pl.DeviceIdType.MESH
F32 = jnp.float32
BF16 = jnp.bfloat16
N = 64
TP = 4
TOK = 128
CHAN = 1024
FFT = 2 * N * TOK
EPS = 1e-05
HALF = CHAN // 2
GROUP = 8


def split_table(table):
    high = table.astype(ml_dtypes.bfloat16)
    low = (table - high.astype(np.float64)).astype(ml_dtypes.bfloat16)
    return high, low


def tables():
    bits = N.bit_length() - 1
    place = np.arange(N)
    rev = np.zeros_like(place)
    for bit in range(bits):
        rev |= (place >> bit & 1) << (bits - 1 - bit)
    residue = np.concatenate([2 * rev, 2 * rev + 1])
    block = np.arange(N)
    pos = np.arange(TOK)
    angle = 2 * np.pi / (2 * N) * ((residue[:, None] * block[None, :]) % (2 * N))
    first = np.concatenate([np.cos(angle), -np.sin(angle)])
    high, low = split_table(first)
    first_cat = np.concatenate([high, high, low], axis=1)
    last = np.concatenate([np.cos(angle), -np.sin(angle)]).T / FFT
    high, low = split_table(last)
    last_cat = np.concatenate([high, high, low], axis=1)
    turn = 2 * np.pi / FFT * ((residue[:, None] * pos[None, :]) % FFT)
    inner = 2 * np.pi / TOK * ((pos[:, None] * pos[None, :]) % TOK)
    cos, sin = np.cos(inner), np.sin(inner)
    forward = np.block([[cos, -sin], [sin, cos]])
    high, low = split_table(forward)
    forward_cat = np.concatenate([high, high, low], axis=0)
    backward = np.block([[cos, sin], [-sin, cos]])
    high, low = split_table(backward)
    backward_cat = np.concatenate([high, high, low], axis=0)
    return (
        first_cat,
        forward_cat,
        backward_cat,
        last_cat,
        np.cos(turn).astype(np.float32),
        np.sin(turn).astype(np.float32),
    )


def parts(value):
    high = value.astype(BF16)
    return high, (value - high.astype(F32)).astype(BF16)


def kernel(
    gate_ref,
    key_ref,
    value_ref,
    real_ref,
    imag_ref,
    gain_ref,
    first_ref,
    forward_ref,
    backward_ref,
    last_ref,
    cos_ref,
    sin_ref,
    out_ref,
    sig_send,
    sig_recv,
    fil_send,
    fil_recv,
    freq,
    rows_wide,
    cols_sig,
    cols_wide,
    res_send,
    res_recv,
    gate_t,
    gated,
    sum_send,
    sum_recv,
    send_sem,
    sig_sem,
    fil_sem,
    res_sem,
    sum_sem,
    own_sem,
):
    me = lax.axis_index("ctx")
    tp = lax.axis_index("tp")
    barrier = pltpu.get_barrier_semaphore()

    def greet(k, carry):
        pl.semaphore_signal(
            barrier, inc=1, device_id={"ctx": (me + k) % N}, device_id_type=MESH
        )
        return carry

    lax.fori_loop(1, N, greet, 0)
    for k in range(1, TP):
        pl.semaphore_signal(
            barrier, inc=1, device_id={"tp": (tp + k) % TP}, device_id_type=MESH
        )

    for j in range(8):
        lanes = pl.ds(j * 128, 128)
        signal = key_ref[:, lanes].astype(F32) * value_ref[:, lanes].astype(F32)
        turned = signal.T
        for i in range(16):
            device = (j % 4) * 16 + i
            sig_send[pl.ds(device * 16 + (j // 4) * 8, 8), :] = turned[i * 8 : i * 8 + 8]

    for j in range(8):
        for e in range(2):
            for part, ref in enumerate((real_ref, imag_ref)):
                turned = ref[pl.ds(j * 2 + e, 128, stride=16), :].T
                for i in range(16):
                    device = (j % 4) * 16 + i
                    row = (((j // 4) * N + device) * 4 + e * 2 + part) * 8
                    fil_send[pl.ds(row, 8), :] = turned[i * 8 : i * 8 + 8]

    pl.semaphore_wait(barrier, N - 1 + TP - 1)

    def send_signal(k, carry):
        peer = (me + k) % N
        pltpu.make_async_remote_copy(
            sig_send.at[pl.ds(peer * 16, 16)],
            sig_recv.at[pl.ds(me * 16, 16)],
            send_sem.at[0],
            sig_sem,
            device_id={"ctx": peer},
            device_id_type=MESH,
        ).start()
        return carry

    lax.fori_loop(1, N, send_signal, 0)

    for h in range(2):

        def send_filter(k, carry):
            peer = (me + k) % N
            pltpu.make_async_remote_copy(
                fil_send.at[pl.ds((h * N + peer) * 32, 32)],
                fil_recv.at[pl.ds((h * N + me) * 32, 32)],
                send_sem.at[1 + h],
                fil_sem.at[h],
                device_id={"ctx": peer},
                device_id_type=MESH,
            ).start()
            return carry

        lax.fori_loop(1, N, send_filter, 0)

    own = [
        pltpu.make_async_copy(
            sig_send.at[pl.ds(me * 16, 16)], sig_recv.at[pl.ds(me * 16, 16)], own_sem.at[0]
        )
    ]
    for h in range(2):
        rows = pl.ds((h * N + me) * 32, 32)
        own.append(
            pltpu.make_async_copy(fil_send.at[rows], fil_recv.at[rows], own_sem.at[1 + h])
        )
    for copy in own:
        copy.start()

    for j in range(8):
        gate_t[pl.ds(j * 128, 128), :] = gate_ref[:, pl.ds(j * 128, 128)].astype(F32).T

    def landed(buffer, rows, sem):
        view = buffer.at[pl.ds(0, rows)]
        pltpu.make_async_copy(view, view, sem).wait()

    own[0].wait()
    landed(sig_recv, (N - 1) * 16, sig_sem)

    for h in range(2):
        for c in range(GROUP):
            high, low = parts(sig_recv[pl.ds(h * 8 + c, N, stride=16), :])
            lanes = pl.ds(c * 128, 128)
            cols_sig[pl.ds(0, N), lanes] = high
            cols_sig[pl.ds(N, N), lanes] = low
            cols_sig[pl.ds(2 * N, N), lanes] = high
        for c in range(GROUP):
            lanes = pl.ds(c * 128, 128)
            mid = jnp.dot(first_ref[...], cols_sig[:, lanes], preferred_element_type=F32)
            re, im = mid[:128], mid[128:]
            cos, sin = cos_ref[...], sin_ref[...]
            rows = pl.ds(c * 128, 128)
            high, low = parts(re * cos + im * sin)
            rows_wide[rows, pl.ds(0, 128)] = high
            rows_wide[rows, pl.ds(256, 128)] = low
            rows_wide[rows, pl.ds(512, 128)] = high
            high, low = parts(im * cos - re * sin)
            rows_wide[rows, pl.ds(128, 128)] = high
            rows_wide[rows, pl.ds(384, 128)] = low
            rows_wide[rows, pl.ds(640, 128)] = high
        for c in range(0, GROUP, 2):
            rows = pl.ds(c * 128, 256)
            freq[pl.ds((h * GROUP + c) * 128, 256), :] = jnp.dot(
                rows_wide[rows, :], forward_ref[...], preferred_element_type=F32
            )

    for h in range(2):
        own[1 + h].wait()
        landed(fil_recv, (N - 1) * 32, fil_sem.at[h])
        for c in range(GROUP):
            for e in range(2):
                base = h * N * 32 + e * 16 + c
                f_re = fil_recv[pl.ds(base, N, stride=32), :]
                f_im = fil_recv[pl.ds(base + 8, N, stride=32), :]
                src = pl.ds((h * GROUP + c) * 128 + e * N, N)
                x_re = freq[src, pl.ds(0, 128)]
                x_im = freq[src, pl.ds(128, 128)]
                rows = pl.ds(c * 128 + e * N, N)
                high, low = parts(x_re * f_re - x_im * f_im)
                rows_wide[rows, pl.ds(0, 128)] = high
                rows_wide[rows, pl.ds(256, 128)] = low
                rows_wide[rows, pl.ds(512, 128)] = high
                high, low = parts(x_re * f_im + x_im * f_re)
                rows_wide[rows, pl.ds(128, 128)] = high
                rows_wide[rows, pl.ds(384, 128)] = low
                rows_wide[rows, pl.ds(640, 128)] = high
        for c in range(0, GROUP, 2):
            rows = pl.ds(c * 128, 256)
            back = jnp.dot(rows_wide[rows, :], backward_ref[...], preferred_element_type=F32)
            cos, sin = cos_ref[...], sin_ref[...]
            for i in range(2):
                lanes = pl.ds((c + i) * 128, 128)
                re = back[i * 128 : i * 128 + 128, :128]
                im = back[i * 128 : i * 128 + 128, 128:]
                high, low = parts(re * cos - im * sin)
                cols_wide[pl.ds(0, 128), lanes] = high
                cols_wide[pl.ds(256, 128), lanes] = low
                cols_wide[pl.ds(512, 128), lanes] = high
                high, low = parts(re * sin + im * cos)
                cols_wide[pl.ds(128, 128), lanes] = high
                cols_wide[pl.ds(384, 128), lanes] = low
                cols_wide[pl.ds(640, 128), lanes] = high
        for c in range(0, GROUP, 2):
            conv = jnp.dot(
                last_ref[...], cols_wide[:, pl.ds(c * 128, 256)], preferred_element_type=F32
            )
            for i in range(2):
                res_send[pl.ds(h * HALF + c + i, N, stride=8), :] = conv[:, i * 128 : i * 128 + 128]

        def send_result(k, carry):
            peer = (me + k) % N
            pltpu.make_async_remote_copy(
                res_send.at[pl.ds(h * HALF + peer * 8, 8)],
                res_recv.at[pl.ds(h * HALF + me * 8, 8)],
                send_sem.at[3 + h],
                res_sem.at[h],
                device_id={"ctx": peer},
                device_id_type=MESH,
            ).start()
            return carry

        lax.fori_loop(1, N, send_result, 0)
        rows = pl.ds(h * HALF + me * 8, 8)
        res_recv[rows, :] = res_send[rows, :]

    total = jnp.zeros((8, 128), F32)
    for h in range(2):
        landed(res_recv, (N - 1) * 8, res_sem.at[h])
        for j in range(4):
            rows = pl.ds(h * HALF + j * 128, 128)
            value = res_recv[rows, :] * gate_t[rows, :]
            gate_t[rows, :] = value
            total = total + jnp.sum((value * value).reshape(16, 8, 128), axis=0)
    total = jnp.broadcast_to(jnp.sum(total, axis=0, keepdims=True), (8, 128))
    sum_send[...] = total
    copies = []
    for k in range(1, TP):
        copies.append(
            pltpu.make_async_remote_copy(
                sum_send,
                sum_recv.at[k],
                send_sem.at[4 + k],
                sum_sem.at[k],
                device_id={"tp": (tp + k) % TP},
                device_id_type=MESH,
            )
        )
    for copy in copies:
        copy.start()
    for j in range(8):
        lanes = pl.ds(j * 128, 128)
        gated[:, lanes] = gate_t[pl.ds(j * 128, 128), :].T * gain_ref[:, lanes]
    for k, copy in enumerate(copies):
        copy.wait()
        total = total + sum_recv[k + 1]
    scale = lax.rsqrt(total / (CHAN * TP) + EPS)
    scale = jnp.broadcast_to(scale[:1], (128, 128)).T
    for j in range(8):
        lanes = pl.ds(j * 128, 128)
        out_ref[:, lanes] = (gated[:, lanes] * scale).astype(BF16)

    landed(sig_send, (N - 1) * 16, send_sem.at[0])
    for h in range(2):
        landed(fil_send, (N - 1) * 32, send_sem.at[1 + h])
        landed(res_send, (N - 1) * 8, send_sem.at[3 + h])


def local(gate_branch, key_branch, value_branch, spectrum_real, spectrum_imag, norm_gain):
    def lines(spectrum):
        split = spectrum.reshape(TOK, 2, CHAN // 128, 128)
        return split.transpose(0, 2, 1, 3).reshape(TOK * 2 * CHAN // 128, 128)

    args = (
        gate_branch,
        key_branch,
        value_branch,
        lines(spectrum_real),
        lines(spectrum_imag),
        norm_gain.reshape(1, CHAN),
    ) + tuple(jnp.asarray(table) for table in tables())
    vmem = pl.BlockSpec(memory_space=pltpu.VMEM)
    return pl.pallas_call(
        kernel,
        out_shape=jax.ShapeDtypeStruct((TOK, CHAN), BF16),
        in_specs=[vmem] * len(args),
        out_specs=vmem,
        scratch_shapes=[
            pltpu.VMEM((CHAN, 128), F32),
            pltpu.VMEM((CHAN, 128), F32),
            pltpu.VMEM((4 * CHAN, 128), F32),
            pltpu.VMEM((4 * CHAN, 128), F32),
            pltpu.VMEM((2 * GROUP * 128, 256), F32),
            pltpu.VMEM((GROUP * 128, 768), BF16),
            pltpu.VMEM((3 * N, GROUP * 128), BF16),
            pltpu.VMEM((768, GROUP * 128), BF16),
            pltpu.VMEM((CHAN, 128), F32),
            pltpu.VMEM((CHAN, 128), F32),
            pltpu.VMEM((CHAN, 128), F32),
            pltpu.VMEM((TOK, CHAN), F32),
            pltpu.VMEM((8, 128), F32),
            pltpu.VMEM((TP, 8, 128), F32),
            pltpu.SemaphoreType.DMA((8,)),
            pltpu.SemaphoreType.DMA,
            pltpu.SemaphoreType.DMA((2,)),
            pltpu.SemaphoreType.DMA((2,)),
            pltpu.SemaphoreType.DMA((TP,)),
            pltpu.SemaphoreType.DMA((3,)),
        ],
        compiler_params=pltpu.CompilerParams(
            collective_id=0, has_side_effects=True, vmem_limit_bytes=48 << 20
        ),
    )(*args)


def solution(mesh):
    in_specs = (
        P("ctx", "tp"),
        P("ctx", "tp"),
        P("ctx", "tp"),
        P(None, "ctx", "tp"),
        P(None, "ctx", "tp"),
        P("tp"),
    )
    return jax.shard_map(
        local, mesh=mesh, in_specs=in_specs, out_specs=P("ctx", "tp"), check_vma=False
    )
```

time: 745 us -> 99.1 us (0.13)
  waiting for transfers between devices: 615 us -> 0 us
  Pallas kernels: 0 us -> 86.5 us
  starting transfers between devices: 56.7 us -> 0 us
  other arithmetic: 42.3 us -> 0 us
  matrix products: 14 us -> 0 us
  local copies, waits for them, and re-layouts: 3.47 us -> 12.2 us
  blocking collectives: 8.53 us -> 0 us
    ppermute x12 -> x0, waiting for transfers between devices: 615 us -> none  [swapped(): lax.ppermute(array, axis, [(i, i ^ 1 << distance) for i in range(lax.axis...]
    pallas_call x0 -> x1, Pallas kernels: none -> 86.5 us  [local(): pl.pallas_call(kernel, out_shape=jax.ShapeDtypeStruct((TOK, CHAN), BF16),...]
    ppermute x12 -> x0, starting transfers between devices: 56.7 us -> none  [swapped(): lax.ppermute(array, axis, [(i, i ^ 1 << distance) for i in range(lax.axis...]
    add x13 -> x0, other arithmetic: 21.6 us -> none  [the longest x6 10.8 us: local(): carried = partner + flip_sign * prepared]
    another operation x14 -> x0, other arithmetic: 17.8 us -> none  [the longest x6 8.8 us: local(): prepared = jnp.stack([prep_real, prep_imag])]
    dot_general x8 -> x0, matrix products: 14 us -> none  [the longest x1 2.16 us: local(): jnp.einsum('bk,kec->ebc', dft_sin, prod_real, precision=highest)]
    unnamed x11 -> x25, local copies, waits for them, and re-layouts: 2.62 us -> 12.2 us
    psum x1 -> x0, blocking collectives: 8.53 us -> none  [local(): channel_total = lax.psum(local_sum, 'tp')]
  transfers between devices with their start and end apart: 12 -> 0, of which waited for: 12 -> 0; matrix products, arithmetic and copies ran while one was open for 0% -> 0% of each run, Pallas kernels for 0% -> 0%
where the time goes in v1:
time: 99.1 us; the launch traced here: 98.6 us
  Pallas kernels  86.5 us (87%)
  local copies, waits for them, and re-layouts  12.2 us (12%)
    pallas_call x1, Pallas kernels, local(): pl.pallas_call(kernel, out_shape=jax.ShapeDtypeStruct((TOK, CHAN), BF16),...  86.5 us
    unnamed x25, local copies, waits for them, and re-layouts  12.2 us

profile of v1, /device:TPU:1, one launch (start us, length us, event | category | flops | bytes accessed | tf_op | source)
XLA Modules:
  0.0 98.6 jit_solution(16214599985610869228)
XLA Ops:
  0.0 0.0 copy-start.11
  0.0 0.7 copy-done.11
  0.7 0.0 copy-start
  0.7 1.2 %copy-done = f32[128,2,1024]{2,1,0:T(2,128)S(1)} copy-done((f32[128,2,1024]{2,1,0:T(2,128)S(1)}, f32[128,2,1024]{2,1,0:T(2,128)}, u32[]{:S(2)}) %copy-start) | copy-done | bytes 1048600
  1.9 0.0 copy-start.1
  1.9 1.2 %copy-done.1 = f32[128,2,1024]{2,1,0:T(2,128)S(1)} copy-done((f32[128,2,1024]{2,1,0:T(2,128)S(1)}, f32[128,2,1024]{2,1,0:T(2,128)}, u32[]{:S(2)}) %copy-start.1) | copy-done | bytes 1048600
  3.1 0.0 copy-start.2
  3.1 1.0 %copy-done.2 = bf16[768,256]{1,0:T(8,128)(2,1)S(1)} copy-done((bf16[768,256]{1,0:T(8,128)(2,1)S(1)}, bf16[768,256]{1,0:T(8,128)(2,1)}, u32[]{:S(2)}) %copy-start.2) | copy-done | bytes 393240
  4.1 0.0 copy-start.3
  4.1 1.0 %copy-done.3 = bf16[768,256]{1,0:T(8,128)(2,1)S(1)} copy-done((bf16[768,256]{1,0:T(8,128)(2,1)S(1)}, bf16[768,256]{1,0:T(8,128)(2,1)}, u32[]{:S(2)}) %copy-start.3) | copy-done | bytes 393240
  5.1 0.0 copy-start.4
  5.1 0.9 copy-done.4
  6.1 0.0 copy-start.5
  6.1 0.9 copy-done.5
  7.0 0.0 copy-start.6
  7.0 0.9 copy-done.6
  8.0 0.0 copy-start.7
  8.0 0.9 copy-done.7
  8.9 0.0 copy-start.8
  8.9 0.9 copy-done.8
  9.8 0.8 copy-done.9
  10.6 0.8 copy-done.10
  11.5 86.5 %shard_map.118 = bf16[128,1024]{1,0:T(8,128)(2,1)S(1)} custom-call(bf16[128,1024]{1,0:T(8,128)(2,1)S(1)} %copy-done.4, bf16[128,1024]{1,0:T(8,128)(2,1)S(1)} %copy-done.5, bf16[128,1024]{1,0:T(8,128)(2,1)S(1)} %copy-done.6, f32[2048,128]{1,0:T(8,128)S(1)} %bitcast.11, f32[2048,128]{1,0:T(8,128)S(1)} %bitcast.12, f32[1,1024]{1,0:T(1,128)S(1)} %bitcast.13, ...), custom_call_target="tpu_custom_call" | custom-call | tf_op jit(solution)/shard_map/pallas_call | solution.py:336
  97.9 0.7 copy.16
  (2 shorter events, 0.0 us)
Async XLA Ops:
  0.0 0.7 copy-start.11
  0.7 1.2 %copy-start = (f32[128,2,1024]{2,1,0:T(2,128)S(1)}, f32[128,2,1024]{2,1,0:T(2,128)}, u32[]{:S(2)}) copy-start(f32[128,2,1024]{2,1,0:T(2,128)} %param.15) | copy-start | bytes 3145732
  1.9 1.2 %copy-start.1 = (f32[128,2,1024]{2,1,0:T(2,128)S(1)}, f32[128,2,1024]{2,1,0:T(2,128)}, u32[]{:S(2)}) copy-start(f32[128,2,1024]{2,1,0:T(2,128)} %param.16) | copy-start | bytes 3145732
  3.1 1.0 %copy-start.2 = (bf16[768,256]{1,0:T(8,128)(2,1)S(1)}, bf16[768,256]{1,0:T(8,128)(2,1)}, u32[]{:S(2)}) copy-start(bf16[768,256]{1,0:T(8,128)(2,1)} %constant.14.clone.backward_ref) | copy-start | bytes 1179652
  4.1 1.0 %copy-start.3 = (bf16[768,256]{1,0:T(8,128)(2,1)S(1)}, bf16[768,256]{1,0:T(8,128)(2,1)}, u32[]{:S(2)}) copy-start(bf16[768,256]{1,0:T(8,128)(2,1)} %constant.13.clone.forward_ref) | copy-start | bytes 1179652
  5.1 0.9 copy-start.4
  6.1 0.9 copy-start.5
  7.0 0.9 copy-start.6
  8.0 0.9 copy-start.7
  8.9 0.9 copy-start.8
  9.8 0.8 copy-start.9
  10.6 0.8 copy-start.10

commit v2 on v1

--- a/solution.py
+++ b/solution.py
@@ -69,6 +69,19 @@
 
 
 def kernel(
+    gate_hbm,
+    key_hbm,
+    value_hbm,
+    real_hbm,
+    imag_hbm,
+    gain_hbm,
+    first_hbm,
+    forward_hbm,
+    backward_hbm,
+    last_hbm,
+    cos_hbm,
+    sin_hbm,
+    out_ref,
     gate_ref,
     key_ref,
     value_ref,
@@ -81,7 +94,6 @@
     last_ref,
     cos_ref,
     sin_ref,
-    out_ref,
     sig_send,
     sig_recv,
     fil_send,
@@ -102,7 +114,27 @@
     res_sem,
     sum_sem,
     own_sem,
+    load_sem,
 ):
+    pairs = (
+        (key_hbm, key_ref),
+        (value_hbm, value_ref),
+        (real_hbm, real_ref),
+        (imag_hbm, imag_ref),
+        (first_hbm, first_ref),
+        (cos_hbm, cos_ref),
+        (sin_hbm, sin_ref),
+        (forward_hbm, forward_ref),
+        (gate_hbm, gate_ref),
+        (backward_hbm, backward_ref),
+        (last_hbm, last_ref),
+        (gain_hbm, gain_ref),
+    )
+    loads = [
+        pltpu.make_async_copy(src, dst, load_sem.at[i]) for i, (src, dst) in enumerate(pairs)
+    ]
+    for load in loads:
+        load.start()
     me = lax.axis_index("ctx")
     tp = lax.axis_index("tp")
     barrier = pltpu.get_barrier_semaphore()
@@ -119,6 +151,8 @@
             barrier, inc=1, device_id={"tp": (tp + k) % TP}, device_id_type=MESH
         )
 
+    loads[0].wait()
+    loads[1].wait()
     for j in range(8):
         lanes = pl.ds(j * 128, 128)
         signal = key_ref[:, lanes].astype(F32) * value_ref[:, lanes].astype(F32)
@@ -127,6 +161,8 @@
             device = (j % 4) * 16 + i
             sig_send[pl.ds(device * 16 + (j // 4) * 8, 8), :] = turned[i * 8 : i * 8 + 8]
 
+    loads[2].wait()
+    loads[3].wait()
     for j in range(8):
         for e in range(2):
             for part, ref in enumerate((real_ref, imag_ref)):
@@ -181,6 +217,8 @@
     for copy in own:
         copy.start()
 
+    for load in loads[4:]:
+        load.wait()
     for j in range(8):
         gate_t[pl.ds(j * 128, 128), :] = gate_ref[:, pl.ds(j * 128, 128)].astype(F32).T
 
@@ -333,12 +371,14 @@
         norm_gain.reshape(1, CHAN),
     ) + tuple(jnp.asarray(table) for table in tables())
     vmem = pl.BlockSpec(memory_space=pltpu.VMEM)
+    hbm = pl.BlockSpec(memory_space=pltpu.HBM)
     return pl.pallas_call(
         kernel,
         out_shape=jax.ShapeDtypeStruct((TOK, CHAN), BF16),
-        in_specs=[vmem] * len(args),
+        in_specs=[hbm] * len(args),
         out_specs=vmem,
-        scratch_shapes=[
+        scratch_shapes=[pltpu.VMEM(arg.shape, arg.dtype) for arg in args]
+        + [
             pltpu.VMEM((CHAN, 128), F32),
             pltpu.VMEM((CHAN, 128), F32),
             pltpu.VMEM((4 * CHAN, 128), F32),
@@ -359,9 +399,10 @@
             pltpu.SemaphoreType.DMA((2,)),
             pltpu.SemaphoreType.DMA((TP,)),
             pltpu.SemaphoreType.DMA((3,)),
+            pltpu.SemaphoreType.DMA((len(args),)),
         ],
         compiler_params=pltpu.CompilerParams(
-            collective_id=0, has_side_effects=True, vmem_limit_bytes=48 << 20
+            collective_id=0, has_side_effects=True, vmem_limit_bytes=62 << 20
         ),
     )(*args)
 

time: 99.1 us -> 89.3 us (0.901)
  local copies, waits for them, and re-layouts: 12.2 us -> 1.67 us
  Pallas kernels: 86.5 us -> 87.5 us
    unnamed x25 -> x1, local copies, waits for them, and re-layouts: 12.2 us -> 1.67 us
    pallas_call x1, Pallas kernels: 86.5 us -> 87.5 us  [local(): pl.pallas_call(kernel, out_shape=jax.ShapeDtypeStruct((TOK, CHAN), BF16),...]
where the time goes in v2:
time: 89.3 us; the launch traced here: 89.2 us
  Pallas kernels  87.5 us (98%)
  local copies, waits for them, and re-layouts  1.67 us (2%)
    pallas_call x1, Pallas kernels, local(): pl.pallas_call(kernel, out_shape=jax.ShapeDtypeStruct((TOK, CHAN), BF16),...  87.5 us

profile of v2, /device:TPU:1, one launch (start us, length us, event | category | flops | bytes accessed | tf_op | source)
XLA Modules:
  0.0 89.2 jit_solution(15080400455739339440)
XLA Ops:
  0.0 87.5 %shard_map.118 = bf16[128,1024]{1,0:T(8,128)(2,1)} custom-call(bf16[128,1024]{1,0:T(8,128)(2,1)} %gate_hbm.1, bf16[128,1024]{1,0:T(8,128)(2,1)} %key_hbm.1, bf16[128,1024]{1,0:T(8,128)(2,1)} %value_hbm.1, f32[2048,128]{1,0:T(8,128)} %bitcast.11, f32[2048,128]{1,0:T(8,128)} %bitcast.12, f32[1,1024]{1,0:T(1,128)} %bitcast.13, ...), custom_call_target="tpu_custom_call" | custom-call | tf_op jit(solution)/shard_map/pallas_call | solution.py:375
  87.5 1.7 %copy.16 = bf16[128,1024]{1,0:T(8,128)(2,1)} copy(bf16[128,1024]{1,0:T(8,128)(2,1)} %shard_map.118) | data formatting | bytes 524288

commit v3 on v2

v3 whole, which is shorter than its diff:
```python
import functools

import jax
import jax.numpy as jnp
import ml_dtypes
import numpy as np
from jax import lax
from jax.experimental import pallas as pl
from jax.experimental.pallas import tpu as pltpu
from jax.sharding import PartitionSpec as P

MESH = pl.DeviceIdType.MESH
F32 = jnp.float32
BF16 = jnp.bfloat16
N = 64
TP = 4
TOK = 128
CHAN = 1024
FFT = 2 * N * TOK
EPS = 1e-05
NY, NZ = 4, 8
NEAR = N // 2
SET = CHAN // N
GC = 4
GROUPS = SET // GC
MORE = 4
AHEAD = 2
LAG = 2


def split_table(table):
    high = table.astype(ml_dtypes.bfloat16)
    low = (table - high.astype(np.float64)).astype(ml_dtypes.bfloat16)
    return high, low


def tables():
    bits = N.bit_length() - 1
    place = np.arange(N)
    rev = np.zeros_like(place)
    for bit in range(bits):
        rev |= (place >> bit & 1) << (bits - 1 - bit)
    pos = np.arange(TOK)
    step, y, core = np.meshgrid(np.arange(4), np.arange(NY), np.arange(2), indexing="ij")

    def devices(plane):
        return ((y * NZ + plane % NZ) * 2 + core).reshape(-1)

    first, last, cos_turn, sin_turn = [], [], [], []
    for z in range(NZ):
        for near, far in (
            (devices(z - step), devices(z + 1 + step)),
            (devices(z + step), devices(z - 1 - step)),
        ):
            block = np.concatenate([near, far])
            residue = np.concatenate([2 * rev[near], 2 * rev[near] + 1])
            angle = 2 * np.pi / (2 * N) * ((residue[:, None] * block[None, :]) % (2 * N))
            table = np.concatenate([np.cos(angle), -np.sin(angle)])
            high, low = split_table(table)
            first.append(np.concatenate([high, high, low], axis=1))
            high, low = split_table(table.T / FFT)
            last.append(np.concatenate([high, high, low], axis=1))
            turn = 2 * np.pi / FFT * ((residue[:, None] * pos[None, :]) % FFT)
            cos_turn.append(np.cos(turn).astype(np.float32))
            sin_turn.append(np.sin(turn).astype(np.float32))

    def by_plane(pieces):
        return np.stack(pieces).reshape(NZ, -1, pieces[0].shape[1])

    inner = 2 * np.pi / TOK * ((pos[:, None] * pos[None, :]) % TOK)
    cos, sin = np.cos(inner), np.sin(inner)
    forward = np.block([[cos, -sin], [sin, cos]])
    high, low = split_table(forward)
    forward_cat = np.concatenate([high, high, low], axis=0)
    backward = np.block([[cos, sin], [-sin, cos]])
    high, low = split_table(backward)
    backward_cat = np.concatenate([high, high, low], axis=0)
    return (
        by_plane(first),
        forward_cat,
        backward_cat,
        by_plane(last),
        by_plane(cos_turn),
        by_plane(sin_turn),
    )


def parts(value):
    high = value.astype(BF16)
    return high, (value - high.astype(F32)).astype(BF16)


def device(y, z, core):
    return ((y + NY) % NY * NZ + (z + NZ) % NZ) * 2 + core % 2


def kernel(
    gate_hbm,
    key_hbm,
    value_hbm,
    real_hbm,
    imag_hbm,
    gain_hbm,
    first_hbm,
    forward_hbm,
    backward_hbm,
    last_hbm,
    cos_hbm,
    sin_hbm,
    out_ref,
    gate_ref,
    key_ref,
    value_ref,
    real_ref,
    imag_ref,
    gain_ref,
    first_ref,
    forward_ref,
    backward_ref,
    last_ref,
    cos_ref,
    sin_ref,
    sig_send,
    sig_recv,
    fil_send,
    fil_recv,
    freq,
    rows_wide,
    cols_sig,
    cols_wide,
    far_send,
    far_recv,
    res_send,
    res_recv,
    gate_t,
    gated,
    sum_send,
    sum_recv,
    sig_send_sem,
    sig_recv_sem,
    pass_send_sem,
    pass_recv_sem,
    fil_send_sem,
    fil_recv_sem,
    far_send_sem,
    far_recv_sem,
    res_send_sem,
    res_recv_sem,
    sum_send_sem,
    sum_recv_sem,
    own_sem,
    load_sem,
):
    me = lax.axis_index("ctx")
    tp = lax.axis_index("tp")
    y, z, core = me // (2 * NZ), me // 2 % NZ, me % 2
    up, down = device(y, z + 1, core), device(y, z - 1, core)
    barrier = pltpu.get_barrier_semaphore()

    pairs = (
        (key_hbm, key_ref),
        (value_hbm, value_ref),
        (real_hbm, real_ref),
        (imag_hbm, imag_ref),
        (first_hbm.at[z], first_ref),
        (cos_hbm.at[z], cos_ref),
        (sin_hbm.at[z], sin_ref),
        (forward_hbm, forward_ref),
        (gate_hbm, gate_ref),
        (backward_hbm, backward_ref),
        (last_hbm.at[z], last_ref),
        (gain_hbm, gain_ref),
    )
    loads = [
        pltpu.make_async_copy(src, dst, load_sem.at[i]) for i, (src, dst) in enumerate(pairs)
    ]
    for load in loads:
        load.start()

    def greet(k, carry):
        step = k % 7
        step = (step + 1) // 2 * (2 * (step % 2) - 1)
        peer = device(y + k // 7 % NY, z + step, core + k // 28)
        pl.semaphore_signal(barrier, inc=1, device_id={"ctx": peer}, device_id_type=MESH)
        return carry

    lax.fori_loop(1, 56, greet, 0)
    for k in range(1, TP):
        pl.semaphore_signal(
            barrier, inc=1, device_id={"tp": (tp + k) % TP}, device_id_type=MESH
        )

    loads[0].wait()
    loads[1].wait()
    for j in range(8):
        lanes = pl.ds(j * 128, 128)
        turned = (key_ref[:, lanes].astype(F32) * value_ref[:, lanes].astype(F32)).T
        for i in range(128 // GC):
            group, chan_set = divmod((j * 128) // GC + i, N)
            sig_send[pl.ds(chan_set * SET + group * GC, GC), :] = turned[i * GC : i * GC + GC]

    loads[2].wait()
    loads[3].wait()
    for j in range(8):
        for e in range(2):
            for part, ref in enumerate((real_ref, imag_ref)):
                turned = ref[pl.ds(j * 2 + e, 128, stride=16), :].T
                for i in range(128 // GC):
                    row = (((j * 128) // GC + i) * 4 + e * 2 + part) * GC
                    fil_send[pl.ds(row, GC), :] = turned[i * GC : i * GC + GC]

    pl.semaphore_wait(barrier, 55 + TP - 1)

    def reach(m):
        step = m % 4
        return y + m // 4 % NY, core + m // 16, step, step * 8 + y * 2 + core

    def send_signal(m, carry):
        to_y, to_core, step, slot = reach(m)
        for side in range(2):
            plane = z + step if side == 0 else z - step
            chan_set = device(to_y, plane - side, to_core)
            pltpu.make_async_remote_copy(
                sig_send.at[pl.ds(chan_set * SET, SET)],
                sig_recv.at[pl.ds((side * N + slot) * SET, SET)],
                sig_send_sem,
                sig_recv_sem,
                device_id={"ctx": device(to_y, plane, to_core)},
                device_id_type=MESH,
            ).start()
        return carry

    lax.fori_loop(1, NEAR, send_signal, 0)

    def send_filter(group):
        def send(m, carry):
            to_y, to_core, step, slot = reach(m)
            for side in range(2):
                plane = z + step if side == 0 else z - step
                chan_set = device(to_y, plane - side, to_core)
                pltpu.make_async_remote_copy(
                    fil_send.at[pl.ds((group * N + chan_set) * 4 * GC, 4 * GC)],
                    fil_recv.at[pl.ds(((group * 2 + side) * NEAR + slot) * 4 * GC, 4 * GC)],
                    fil_send_sem.at[group],
                    fil_recv_sem.at[group],
                    device_id={"ctx": device(to_y, plane, to_core)},
                    device_id_type=MESH,
                ).start()
            return carry

        lax.fori_loop(1, NEAR, send, 0)

    for group in range(AHEAD):
        send_filter(group)

    sets = (me, down)
    own_slot = y * 2 + core
    own_signal, own_filter = [], []
    for side in range(2):
        own_signal.append(
            pltpu.make_async_copy(
                sig_send.at[pl.ds(sets[side] * SET, SET)],
                sig_recv.at[pl.ds((side * N + own_slot) * SET, SET)],
                own_sem.at[side],
            )
        )
        for group in range(GROUPS):
            own_filter.append(
                pltpu.make_async_copy(
                    fil_send.at[pl.ds((group * N + sets[side]) * 4 * GC, 4 * GC)],
                    fil_recv.at[pl.ds(((group * 2 + side) * NEAR + own_slot) * 4 * GC, 4 * GC)],
                    own_sem.at[2 + side * GROUPS + group],
                )
            )
    for copy in own_signal + own_filter:
        copy.start()

    for load in loads[4:]:
        load.wait()
    for j in range(8):
        gate_t[pl.ds(j * 128, 128), :] = gate_ref[:, pl.ds(j * 128, 128)].astype(F32).T

    def landed(buffer, rows, sem):
        view = buffer.at[pl.ds(0, rows)]
        pltpu.make_async_copy(view, view, sem).wait()

    for copy in own_signal:
        copy.wait()
    landed(sig_recv, 2 * (NEAR - 1) * SET, sig_recv_sem)
    passes = [
        pltpu.make_async_remote_copy(
            sig_recv.at[pl.ds(side * N * SET, NEAR * SET)],
            sig_recv.at[pl.ds(((1 - side) * N + NEAR) * SET, NEAR * SET)],
            pass_send_sem.at[side],
            pass_recv_sem.at[1 - side],
            device_id={"ctx": (up, down)[side]},
            device_id_type=MESH,
        )
        for side in range(2)
    ]
    for copy in passes:
        copy.start()
    for group in range(AHEAD, MORE):
        send_filter(group)
    for side in range(2):
        far = sig_recv.at[pl.ds((side * N + NEAR) * SET, NEAR * SET)]
        pltpu.make_async_copy(far, far, pass_recv_sem.at[side]).wait()

    for side in range(2):
        for c in range(SET):
            high, low = parts(sig_recv[pl.ds(side * N * SET + c, N, stride=SET), :])
            lanes = pl.ds(c * 128, 128)
            cols_sig[pl.ds(0, N), lanes] = high
            cols_sig[pl.ds(N, N), lanes] = low
            cols_sig[pl.ds(2 * N, N), lanes] = high
        cos, sin = cos_ref[pl.ds(side * N, N), :], sin_ref[pl.ds(side * N, N), :]
        for pair in range(SET // 2):
            mid = jnp.dot(
                first_ref[pl.ds(side * 128, 128), :],
                cols_sig[:, pl.ds(pair * 256, 256)],
                preferred_element_type=F32,
            )
            for i in range(2):
                re, im = mid[:N, i * 128 : i * 128 + 128], mid[N:, i * 128 : i * 128 + 128]
                rows = pl.ds((pair * 2 + i) * N, N)
                high, low = parts(re * cos + im * sin)
                rows_wide[rows, pl.ds(0, 128)] = high
                rows_wide[rows, pl.ds(256, 128)] = low
                rows_wide[rows, pl.ds(512, 128)] = high
                high, low = parts(im * cos - re * sin)
                rows_wide[rows, pl.ds(128, 128)] = high
                rows_wide[rows, pl.ds(384, 128)] = low
                rows_wide[rows, pl.ds(640, 128)] = high
        for quad in range(SET // 4):
            freq[pl.ds((side * SET + quad * 4) * N, 4 * N), :] = jnp.dot(
                rows_wide[pl.ds(quad * 4 * N, 4 * N), :],
                forward_ref[...],
                preferred_element_type=F32,
            )

    far_rows = NEAR * GC

    def inverse(group):
        for side in range(2):
            own_filter[side * GROUPS + group].wait()
        landed(fil_recv, 2 * (NEAR - 1) * 4 * GC, fil_recv_sem.at[group])
        for side in range(2):
            for c in range(GC):
                for e in range(2):
                    base = (group * 2 + side) * NEAR * 4 * GC + e * 2 * GC + c
                    f_re = fil_recv[pl.ds(base, NEAR, stride=4 * GC), :]
                    f_im = fil_recv[pl.ds(base + GC, NEAR, stride=4 * GC), :]
                    src = pl.ds((side * SET + group * GC + c) * N + e * NEAR, NEAR)
                    x_re = freq[src, pl.ds(0, 128)]
                    x_im = freq[src, pl.ds(128, 128)]
                    rows = pl.ds((side * GC + c) * N + e * NEAR, NEAR)
                    high, low = parts(x_re * f_re - x_im * f_im)
                    rows_wide[rows, pl.ds(0, 128)] = high
                    rows_wide[rows, pl.ds(256, 128)] = low
                    rows_wide[rows, pl.ds(512, 128)] = high
                    high, low = parts(x_re * f_im + x_im * f_re)
                    rows_wide[rows, pl.ds(128, 128)] = high
                    rows_wide[rows, pl.ds(384, 128)] = low
                    rows_wide[rows, pl.ds(640, 128)] = high
        for quad in range(2 * GC // 4):
            back = jnp.dot(
                rows_wide[pl.ds(quad * 4 * N, 4 * N), :],
                backward_ref[...],
                preferred_element_type=F32,
            )
            for i in range(4):
                side, c = divmod(quad * 4 + i, GC)
                lanes = pl.ds((side * GC + c) * 128, 128)
                cos, sin = cos_ref[pl.ds(side * N, N), :], sin_ref[pl.ds(side * N, N), :]
                re, im = back[i * N : i * N + N, :128], back[i * N : i * N + N, 128:]
                high, low = parts(re * cos - im * sin)
                cols_wide[pl.ds(0, N), lanes] = high
                cols_wide[pl.ds(2 * N, N), lanes] = low
                cols_wide[pl.ds(4 * N, N), lanes] = high
                high, low = parts(re * sin + im * cos)
                cols_wide[pl.ds(N, N), lanes] = high
                cols_wide[pl.ds(3 * N, N), lanes] = low
                cols_wide[pl.ds(5 * N, N), lanes] = high
        for side in range(2):
            for pair in range(GC // 2):
                conv = jnp.dot(
                    last_ref[pl.ds(side * N, N), :],
                    cols_wide[:, pl.ds((side * GC + pair * 2) * 128, 256)],
                    preferred_element_type=F32,
                )
                for i in range(2):
                    base = (group * 2 + side) * far_rows + pair * 2 + i
                    rows = pl.ds(base, NEAR, stride=GC)
                    res_send[rows, :] = conv[:NEAR, i * 128 : i * 128 + 128]
                    far_send[rows, :] = conv[NEAR:, i * 128 : i * 128 + 128]

    def far_copies(group):
        return [
            pltpu.make_async_remote_copy(
                far_send.at[pl.ds((group * 2 + side) * far_rows, far_rows)],
                far_recv.at[pl.ds((group * 2 + 1 - side) * far_rows, far_rows)],
                far_send_sem.at[group * 2 + side],
                far_recv_sem.at[group * 2 + 1 - side],
                device_id={"ctx": (up, down)[side]},
                device_id_type=MESH,
            )
            for side in range(2)
        ]

    own_result = []

    def finish(group):
        for side in range(2):
            rows = pl.ds((group * 2 + side) * far_rows, far_rows)
            view = far_recv.at[rows]
            pltpu.make_async_copy(view, view, far_recv_sem.at[group * 2 + side]).wait()
            res_send[rows, :] = res_send[rows, :] + far_recv[rows, :]

        def send(m, carry):
            step = m % 4
            to_y, to_core = (y + m // 4) % NY, (core + m // 16) % 2
            slot = step * 8 + to_y * 2 + to_core
            for side in range(2):
                plane = z - step if side == 0 else z + step
                pltpu.make_async_remote_copy(
                    res_send.at[pl.ds(((group * 2 + side) * NEAR + slot) * GC, GC)],
                    res_recv.at[pl.ds((group * N + sets[side]) * GC, GC)],
                    res_send_sem.at[group],
                    res_recv_sem.at[group],
                    device_id={"ctx": device(to_y, plane, to_core)},
                    device_id_type=MESH,
                ).start()
            return carry

        lax.fori_loop(1, NEAR, send, 0)
        for side in range(2):
            copy = pltpu.make_async_copy(
                res_send.at[pl.ds(((group * 2 + side) * NEAR + own_slot) * GC, GC)],
                res_recv.at[pl.ds((group * N + sets[side]) * GC, GC)],
                own_sem.at[side],
            )
            copy.start()
            own_result.append(copy)

    for group in range(GROUPS):
        inverse(group)
        for copy in far_copies(group):
            copy.start()
        if group + MORE < GROUPS:
            send_filter(group + MORE)
        if group >= LAG:
            finish(group - LAG)
    for group in range(GROUPS - LAG, GROUPS):
        finish(group)

    for side in range(2):
        view = res_send.at[pl.ds(0, GROUPS * GC)]
        pltpu.make_async_copy(view, view, own_sem.at[side]).wait()
    total = jnp.zeros((8, 128), F32)
    for group in range(GROUPS):
        landed(res_recv, 2 * (NEAR - 1) * GC, res_recv_sem.at[group])
        for j in range(N * GC // 128):
            rows = pl.ds(group * N * GC + j * 128, 128)
            value = res_recv[rows, :] * gate_t[rows, :]
            gate_t[rows, :] = value
            total = total + jnp.sum((value * value).reshape(16, 8, 128), axis=0)
    total = jnp.broadcast_to(jnp.sum(total, axis=0, keepdims=True), (8, 128))
    sum_send[...] = total
    copies = []
    for k in range(1, TP):
        copies.append(
            pltpu.make_async_remote_copy(
                sum_send,
                sum_recv.at[k],
                sum_send_sem.at[k],
                sum_recv_sem.at[k],
                device_id={"tp": (tp + k) % TP},
                device_id_type=MESH,
            )
        )
    for copy in copies:
        copy.start()
    for j in range(8):
        lanes = pl.ds(j * 128, 128)
        gated[:, lanes] = gate_t[pl.ds(j * 128, 128), :].T * gain_ref[:, lanes]
    for k, copy in enumerate(copies):
        copy.wait()
        total = total + sum_recv[k + 1]
    scale = lax.rsqrt(total / (CHAN * TP) + EPS)
    scale = jnp.broadcast_to(scale[:1], (128, 128)).T
    for j in range(8):
        lanes = pl.ds(j * 128, 128)
        out_ref[:, lanes] = (gated[:, lanes] * scale).astype(BF16)

    landed(sig_send, 2 * (NEAR - 1) * SET, sig_send_sem)
    for copy in passes:
        copy.wait_send()
    for group in range(GROUPS):
        landed(fil_send, 2 * (NEAR - 1) * 4 * GC, fil_send_sem.at[group])
        for copy in far_copies(group):
            copy.wait_send()
        landed(res_send, 2 * (NEAR - 1) * GC, res_send_sem.at[group])


def local(gate_branch, key_branch, value_branch, spectrum_real, spectrum_imag, norm_gain):
    def lines(spectrum):
        split = spectrum.reshape(TOK, 2, CHAN // 128, 128)
        return split.transpose(0, 2, 1, 3).reshape(TOK * 2 * CHAN // 128, 128)

    args = (
        gate_branch,
        key_branch,
        value_branch,
        lines(spectrum_real),
        lines(spectrum_imag),
        norm_gain.reshape(1, CHAN),
    ) + tuple(jnp.asarray(table) for table in tables())
    vmem = pl.BlockSpec(memory_space=pltpu.VMEM)
    hbm = pl.BlockSpec(memory_space=pltpu.HBM)
    return pl.pallas_call(
        kernel,
        out_shape=jax.ShapeDtypeStruct((TOK, CHAN), BF16),
        in_specs=[hbm] * len(args),
        out_specs=vmem,
        scratch_shapes=[pltpu.VMEM(arg.shape[-2:], arg.dtype) for arg in args]
        + [
            pltpu.VMEM((CHAN, 128), F32),
            pltpu.VMEM((2 * CHAN, 128), F32),
            pltpu.VMEM((4 * CHAN, 128), F32),
            pltpu.VMEM((4 * CHAN, 128), F32),
            pltpu.VMEM((2 * SET * N, 256), F32),
            pltpu.VMEM((SET * N, 768), BF16),
            pltpu.VMEM((3 * N, SET * 128), BF16),
            pltpu.VMEM((6 * N, 2 * GC * 128), BF16),
            pltpu.VMEM((CHAN, 128), F32),
            pltpu.VMEM((CHAN, 128), F32),
            pltpu.VMEM((CHAN, 128), F32),
            pltpu.VMEM((CHAN, 128), F32),
            pltpu.VMEM((CHAN, 128), F32),
            pltpu.VMEM((TOK, CHAN), F32),
            pltpu.VMEM((8, 128), F32),
            pltpu.VMEM((TP, 8, 128), F32),
            pltpu.SemaphoreType.DMA,
            pltpu.SemaphoreType.DMA,
            pltpu.SemaphoreType.DMA((2,)),
            pltpu.SemaphoreType.DMA((2,)),
            pltpu.SemaphoreType.DMA((GROUPS,)),
            pltpu.SemaphoreType.DMA((GROUPS,)),
            pltpu.SemaphoreType.DMA((2 * GROUPS,)),
            pltpu.SemaphoreType.DMA((2 * GROUPS,)),
            pltpu.SemaphoreType.DMA((GROUPS,)),
            pltpu.SemaphoreType.DMA((GROUPS,)),
            pltpu.SemaphoreType.DMA((TP,)),
            pltpu.SemaphoreType.DMA((TP,)),
            pltpu.SemaphoreType.DMA((2 + 2 * GROUPS,)),
            pltpu.SemaphoreType.DMA((len(args),)),
        ],
        compiler_params=pltpu.CompilerParams(
            collective_id=0, has_side_effects=True, vmem_limit_bytes=62 << 20
        ),
    )(*args)


def solution(mesh):
    in_specs = (
        P("ctx", "tp"),
        P("ctx", "tp"),
        P("ctx", "tp"),
        P(None, "ctx", "tp"),
        P(None, "ctx", "tp"),
        P("tp"),
    )
    return jax.shard_map(
        local, mesh=mesh, in_specs=in_specs, out_specs=P("ctx", "tp"), check_vma=False
    )
```

time: 89.3 us -> 85 us (0.952)
  Pallas kernels: 87.5 us -> 83.2 us
    pallas_call x1, Pallas kernels: 87.5 us -> 83.2 us  [local(): pl.pallas_call(kernel, out_shape=jax.ShapeDtypeStruct((TOK, CHAN), BF16),...]
where the time goes in v3:
time: 85 us; the launch traced here: 84.9 us
  Pallas kernels  83.2 us (98%)
  local copies, waits for them, and re-layouts  1.67 us (2%)
    pallas_call x1, Pallas kernels, local(): pl.pallas_call(kernel, out_shape=jax.ShapeDtypeStruct((TOK, CHAN), BF16),...  83.2 us

profile of v3, /device:TPU:1, one launch (start us, length us, event | category | flops | bytes accessed | tf_op | source)
XLA Modules:
  0.0 84.9 jit_solution(11777553312389557333)
XLA Ops:
  0.0 83.2 %shard_map.118 = bf16[128,1024]{1,0:T(8,128)(2,1)} custom-call(bf16[128,1024]{1,0:T(8,128)(2,1)} %gate_hbm.1, bf16[128,1024]{1,0:T(8,128)(2,1)} %key_hbm.1, bf16[128,1024]{1,0:T(8,128)(2,1)} %value_hbm.1, f32[2048,128]{1,0:T(8,128)} %bitcast.11, f32[2048,128]{1,0:T(8,128)} %bitcast.12, f32[1,1024]{1,0:T(1,128)} %bitcast.13, ...), custom_call_target="tpu_custom_call" | custom-call | tf_op jit(solution)/shard_map/pallas_call | solution.py:520
  83.2 1.7 %copy.16 = bf16[128,1024]{1,0:T(8,128)(2,1)} copy(bf16[128,1024]{1,0:T(8,128)(2,1)} %shard_map.118) | data formatting | bytes 524288

commit v4 on v3

--- a/solution.py
+++ b/solution.py
@@ -23,6 +23,7 @@
 SET = CHAN // N
 GC = 4
 GROUPS = SET // GC
+GROUP_TILES = N * GC // 128
 MORE = 4
 AHEAD = 2
 LAG = 2
@@ -91,7 +92,7 @@
 
 
 def device(y, z, core):
-    return ((y + NY) % NY * NZ + (z + NZ) % NZ) * 2 + core % 2
+    return (y % NY * NZ + (z + NZ) % NZ) * 2 + core % 2
 
 
 def kernel(
@@ -157,6 +158,19 @@
     up, down = device(y, z + 1, core), device(y, z - 1, core)
     barrier = pltpu.get_barrier_semaphore()
 
+    def greet(k, carry):
+        step = k % 7
+        step = (step + 1) // 2 * (2 * (step % 2) - 1)
+        peer = device(y + k // 7 % NY, z + step, core + k // 28)
+        pl.semaphore_signal(barrier, inc=1, device_id={"ctx": peer}, device_id_type=MESH)
+        return carry
+
+    lax.fori_loop(1, 56, greet, 0)
+    for k in range(1, TP):
+        pl.semaphore_signal(
+            barrier, inc=1, device_id={"tp": (tp + k) % TP}, device_id_type=MESH
+        )
+
     pairs = (
         (key_hbm, key_ref),
         (value_hbm, value_ref),
@@ -177,19 +191,6 @@
     for load in loads:
         load.start()
 
-    def greet(k, carry):
-        step = k % 7
-        step = (step + 1) // 2 * (2 * (step % 2) - 1)
-        peer = device(y + k // 7 % NY, z + step, core + k // 28)
-        pl.semaphore_signal(barrier, inc=1, device_id={"ctx": peer}, device_id_type=MESH)
-        return carry
-
-    lax.fori_loop(1, 56, greet, 0)
-    for k in range(1, TP):
-        pl.semaphore_signal(
-            barrier, inc=1, device_id={"tp": (tp + k) % TP}, device_id_type=MESH
-        )
-
     loads[0].wait()
     loads[1].wait()
     for j in range(8):
@@ -199,21 +200,11 @@
             group, chan_set = divmod((j * 128) // GC + i, N)
             sig_send[pl.ds(chan_set * SET + group * GC, GC), :] = turned[i * GC : i * GC + GC]
 
-    loads[2].wait()
-    loads[3].wait()
-    for j in range(8):
-        for e in range(2):
-            for part, ref in enumerate((real_ref, imag_ref)):
-                turned = ref[pl.ds(j * 2 + e, 128, stride=16), :].T
-                for i in range(128 // GC):
-                    row = (((j * 128) // GC + i) * 4 + e * 2 + part) * GC
-                    fil_send[pl.ds(row, GC), :] = turned[i * GC : i * GC + GC]
-
     pl.semaphore_wait(barrier, 55 + TP - 1)
 
     def reach(m):
-        step = m % 4
-        return y + m // 4 % NY, core + m // 16, step, step * 8 + y * 2 + core
+        step = (m % 4 + m // 4) % 4
+        return y + m % 4, core + m // 16, step, step * 8 + y * 2 + core
 
     def send_signal(m, carry):
         to_y, to_core, step, slot = reach(m)
@@ -231,6 +222,15 @@
         return carry
 
     lax.fori_loop(1, NEAR, send_signal, 0)
+
+    def turn_filter(group):
+        for j in range(group * GROUP_TILES, (group + 1) * GROUP_TILES):
+            for e in range(2):
+                for part, ref in enumerate((real_ref, imag_ref)):
+                    turned = ref[pl.ds(j * 2 + e, 128, stride=16), :].T
+                    for i in range(128 // GC):
+                        row = (((j * 128) // GC + i) * 4 + e * 2 + part) * GC
+                        fil_send[pl.ds(row, GC), :] = turned[i * GC : i * GC + GC]
 
     def send_filter(group):
         def send(m, carry):
@@ -250,8 +250,12 @@
 
         lax.fori_loop(1, NEAR, send, 0)
 
-    for group in range(AHEAD):
-        send_filter(group)
+    loads[2].wait()
+    loads[3].wait()
+    for group in range(GROUPS):
+        turn_filter(group)
+        if group < AHEAD:
+            send_filter(group)
 
     sets = (me, down)
     own_slot = y * 2 + core
@@ -417,8 +421,8 @@
             res_send[rows, :] = res_send[rows, :] + far_recv[rows, :]
 
         def send(m, carry):
-            step = m % 4
-            to_y, to_core = (y + m // 4) % NY, (core + m // 16) % 2
+            step = (m % 4 + m // 4) % 4
+            to_y, to_core = (y + m % 4) % NY, (core + m // 16) % 2
             slot = step * 8 + to_y * 2 + to_core
             for side in range(2):
                 plane = z - step if side == 0 else z + step
@@ -432,7 +436,7 @@
                 ).start()
             return carry
 
-        lax.fori_loop(1, NEAR, send, 0)
+        lax.fori_loop(1, NEAR, send, 0, unroll=True)
         for side in range(2):
             copy = pltpu.make_async_copy(
                 res_send.at[pl.ds(((group * 2 + side) * NEAR + own_slot) * GC, GC)],

time: 85 us -> 84 us (0.988)
  Pallas kernels: 83.2 us -> 82.2 us
    pallas_call x1, Pallas kernels: 83.2 us -> 82.2 us  [local(): pl.pallas_call(kernel, out_shape=jax.ShapeDtypeStruct((TOK, CHAN), BF16),...]
where the time goes in v4:
time: 84 us; the launch traced here: 83.9 us
  Pallas kernels  82.2 us (98%)
  local copies, waits for them, and re-layouts  1.67 us (2%)
    pallas_call x1, Pallas kernels, local(): pl.pallas_call(kernel, out_shape=jax.ShapeDtypeStruct((TOK, CHAN), BF16),...  82.2 us

profile of v4, /device:TPU:1, one launch (start us, length us, event | category | flops | bytes accessed | tf_op | source)
XLA Modules:
  0.0 83.9 jit_solution(10898572396934373238)
XLA Ops:
  0.0 82.2 %shard_map.118 = bf16[128,1024]{1,0:T(8,128)(2,1)} custom-call(bf16[128,1024]{1,0:T(8,128)(2,1)} %gate_hbm.1, bf16[128,1024]{1,0:T(8,128)(2,1)} %key_hbm.1, bf16[128,1024]{1,0:T(8,128)(2,1)} %value_hbm.1, f32[2048,128]{1,0:T(8,128)} %bitcast.11, f32[2048,128]{1,0:T(8,128)} %bitcast.12, f32[1,1024]{1,0:T(1,128)} %bitcast.13, ...), custom_call_target="tpu_custom_call" | custom-call | tf_op jit(solution)/shard_map/pallas_call | solution.py:524
  82.2 1.7 %copy.16 = bf16[128,1024]{1,0:T(8,128)(2,1)} copy(bf16[128,1024]{1,0:T(8,128)(2,1)} %shard_map.118) | data formatting | bytes 524288

commit v5 on v4

--- a/solution.py
+++ b/solution.py
@@ -135,6 +135,7 @@
     res_recv,
     gate_t,
     gated,
+    mixed,
     sum_send,
     sum_recv,
     sig_send_sem,
@@ -492,10 +493,18 @@
         total = total + sum_recv[k + 1]
     scale = lax.rsqrt(total / (CHAN * TP) + EPS)
     scale = jnp.broadcast_to(scale[:1], (128, 128)).T
-    for j in range(8):
-        lanes = pl.ds(j * 128, 128)
-        out_ref[:, lanes] = (gated[:, lanes] * scale).astype(BF16)
-
+    stores = []
+    for j in range(4):
+        lanes = pl.ds(j * 256, 256)
+        wide = jnp.concatenate([scale, scale], axis=1)
+        mixed[:, lanes] = (gated[:, lanes] * wide).astype(BF16)
+        stores.append(
+            pltpu.make_async_copy(mixed.at[:, lanes], out_ref.at[:, lanes], load_sem.at[j])
+        )
+        stores[-1].start()
+
+    for store in stores:
+        store.wait()
     landed(sig_send, 2 * (NEAR - 1) * SET, sig_send_sem)
     for copy in passes:
         copy.wait_send()
@@ -519,13 +528,12 @@
         lines(spectrum_imag),
         norm_gain.reshape(1, CHAN),
     ) + tuple(jnp.asarray(table) for table in tables())
-    vmem = pl.BlockSpec(memory_space=pltpu.VMEM)
     hbm = pl.BlockSpec(memory_space=pltpu.HBM)
     return pl.pallas_call(
         kernel,
         out_shape=jax.ShapeDtypeStruct((TOK, CHAN), BF16),
         in_specs=[hbm] * len(args),
-        out_specs=vmem,
+        out_specs=hbm,
         scratch_shapes=[pltpu.VMEM(arg.shape[-2:], arg.dtype) for arg in args]
         + [
             pltpu.VMEM((CHAN, 128), F32),
@@ -542,6 +550,7 @@
             pltpu.VMEM((CHAN, 128), F32),
             pltpu.VMEM((CHAN, 128), F32),
             pltpu.VMEM((TOK, CHAN), F32),
+            pltpu.VMEM((TOK, CHAN), BF16),
             pltpu.VMEM((8, 128), F32),
             pltpu.VMEM((TP, 8, 128), F32),
             pltpu.SemaphoreType.DMA,

time: 84 us -> 84 us (level)
  no operation moved by 1% of the time
where the time goes in v5:
time: 84 us; the launch traced here: 83.9 us
  Pallas kernels  82.2 us (98%)
  local copies, waits for them, and re-layouts  1.67 us (2%)
    pallas_call x1, Pallas kernels, local(): pl.pallas_call(kernel, out_shape=jax.ShapeDtypeStruct((TOK, CHAN), BF16),...  82.2 us

profile of v5, /device:TPU:1, one launch (start us, length us, event | category | flops | bytes accessed | tf_op | source)
XLA Modules:
  0.0 83.9 jit_solution(17906352252062497180)
XLA Ops:
  0.0 82.2 %shard_map.118 = bf16[128,1024]{1,0:T(8,128)(2,1)} custom-call(bf16[128,1024]{1,0:T(8,128)(2,1)} %gate_hbm.1, bf16[128,1024]{1,0:T(8,128)(2,1)} %key_hbm.1, bf16[128,1024]{1,0:T(8,128)(2,1)} %value_hbm.1, f32[2048,128]{1,0:T(8,128)} %bitcast.11, f32[2048,128]{1,0:T(8,128)} %bitcast.12, f32[1,1024]{1,0:T(1,128)} %bitcast.13, ...), custom_call_target="tpu_custom_call" | custom-call | tf_op jit(solution)/shard_map/pallas_call | solution.py:532
  82.2 1.7 %copy.16 = bf16[128,1024]{1,0:T(8,128)(2,1)} copy(bf16[128,1024]{1,0:T(8,128)(2,1)} %shard_map.118) | data formatting | bytes 524288
